TPU v7x, 256 devices: a whole 4x4x8 slice. The times are simulated.
256 devices in a mesh: group: 4 (over y), region: 64 (over x, z, core).
Axes of the slice: x: 4, y: 4, z: 8, core: 2. Of those that a mesh axis runs over, the one named last changes fastest.
Arguments:
- position: float32 [3, 262144], P(None, ('group', 'region')), may hold values from -6 to 6
- velocity: float32 [3, 262144], P(None, ('group', 'region')), may hold values from -6 to 6
- accel_old: float32 [3, 262144], P(None, ('group', 'region')), may hold values from -6 to 6
- orientation: float32 [9, 262144], P(None, ('group', 'region')), may hold values from -3.5 to 3.5
- spin: float32 [3, 262144], P(None, ('group', 'region')), may hold values from -6 to 6
- shape_index: int32 [262144], P(('group', 'region')), may hold values from 0 to 63
- shape_offsets: float32 [64, 3, 128], replicated, may hold values from -3 to 3
- shape_radii: float32 [64, 128], replicated, may hold values from 0.2 to 0.6
- pair_first: int32 [32768], P(('group', 'region')), may hold values from 0 to 1023
- pair_second: int32 [32768], P(('group', 'region')), may hold values from 0 to 1278
- pair_neck: float32 [32768], P(('group', 'region')), may hold values from 0.05 to 0.5
- cross_first: int32 [16384], P(('group', 'region')), may hold values from 0 to 1023
- cross_second: int32 [16384], P(('group', 'region')), may hold values from 0 to 127
- cross_neck: float32 [16384], P(('group', 'region')), may hold values from 0.05 to 0.5
- export_slots: int32 [32768], P(('group', 'region')), may hold values from 0 to 1023
Outputs:
- moved: float32 [3, 262144], P(None, ('group', 'region'))
- velocity_new: float32 [3, 262144], P(None, ('group', 'region'))
- spin_new: float32 [3, 262144], P(None, ('group', 'region'))
All inputs are finite; a program needn't handle non-finite values.
Results may differ from a plain program's by a relative error of at most 0.00002.
Values sent between devices are 32-bit elements; how exact they have to be, the bound alone decides.
No kernel may reach another device: no remote copies, remote signals or barrier semaphores. Data moves between devices by JAX's collectives and lax.ppermute only.
A program may use at most 64 MiB of HBM per device.

v0:
```python
import functools
import math

import jax
import jax.numpy as jnp
from jax import lax
from jax.experimental import pallas as pl
from jax.experimental.pallas import tpu as pltpu
from jax.sharding import PartitionSpec as P

F32 = jnp.float32
BF16 = jnp.bfloat16
I32 = jnp.int32

BOUND_DEV = 128
CX = 32
KINDS = 64
SUB = 128
GRAINS_DEV = 1024
LANES = 128
HALVES = 2
WIDTH = HALVES * LANES

time_step = 0.05
stiffness = 0.0078125
cohesion = 0.05
inertia = 0.4

SCALE = math.sqrt(math.log2(math.e) / 4)
SOFT = 0.01 * SCALE * SCALE
LIFT = 2.0**SOFT
GAIN = LIFT * SCALE * stiffness
BOND = LIFT * SCALE * cohesion
DRAG = LIFT * stiffness


def iota(shape, dim):
    return lax.broadcasted_iota(I32, shape, dim)


def thirds(x):
    hi = x.astype(BF16).astype(F32)
    rest = x - hi
    mid = rest.astype(BF16).astype(F32)
    return jnp.concatenate([hi, mid, rest - mid], 0).astype(BF16)


def joined(y):
    n = y.shape[0] // 3
    return (y[2 * n :] + y[n : 2 * n]) + y[:n]


def dot(a, b):
    return lax.dot_general(a, b, (((1,), (0,)), ((), ())), preferred_element_type=F32)


def dot_t(a, b):
    return lax.dot_general(a, b, (((1,), (1,)), ((), ())), preferred_element_type=F32)


def hot(index, count):
    return jnp.where(iota((count, index.shape[1]), 0) == index, 1.0, 0.0).astype(BF16)


def wide(row):
    return jnp.concatenate([row, jnp.zeros((1, LANES - row.shape[1]), row.dtype)], 1)


def stack(rows, count):
    at = iota((count, rows[0].shape[1]), 0)
    out = jnp.zeros((count, rows[0].shape[1]), F32)
    for k, row in enumerate(rows):
        out = jnp.where(at == k, row, out)
    return out


def compact(actives, fields):
    segments = len(actives)
    flags = stack([a.astype(F32) for a in actives], 16)
    below = jnp.where(iota((LANES, LANES), 0) < iota((LANES, LANES), 1), 1.0, 0.0).astype(BF16)
    inside = dot(flags.astype(BF16), below)
    sums = dot(flags.astype(BF16), jnp.ones((LANES, LANES), BF16))
    ranks = []
    before = jnp.zeros((1, LANES), F32)
    for s in range(segments):
        ranks.append(jnp.where(actives[s], inside[s : s + 1] + before, -1.0).astype(I32))
        before = before + sums[s : s + 1]
    total = jnp.sum(flags).astype(I32)
    parts = thirds(jnp.concatenate([stack(f, 16) for f in fields], 1))
    return jnp.concatenate(ranks, 1), parts, total


def picked(ranks, parts, base):
    want = iota((WIDTH, ranks.shape[1]), 0) + base
    chosen = jnp.where(want == ranks, 1.0, 0.0).astype(BF16)
    return joined(dot_t(parts, chosen))


def worlds(table_ref, pose):
    at = iota((4 * KINDS, pose.shape[1]), 0)
    kinds = jnp.where(((at & (KINDS - 1)) == pose[12:13].astype(I32)) & (at < 3 * KINDS), 1.0, 0.0).astype(BF16)
    shapes = dot(table_ref[...], kinds)
    offset = [shapes[e * SUB : (e + 1) * SUB] for e in range(4)]
    turn = [SCALE * pose[3 + n : 4 + n] for n in range(9)]
    return [
        turn[3 * c] * offset[0] + turn[3 * c + 1] * offset[1] + turn[3 * c + 2] * offset[2] for c in range(3)
    ] + [GAIN * offset[3]]


def interact(u, v_ref):
    def step(b, sums):
        v = [v_ref[c, pl.ds(b, 8, stride=0), :] for c in range(4)]
        out = []
        for one, s in zip(u, sums):
            x, y, z = (one[c] - v[c] for c in range(3))
            square = (x * x + SOFT) + y * y + z * z
            m = ((one[3] + v[3]) * lax.rsqrt(square) - DRAG) * jnp.exp2(-square)
            out.append((s[0] + m * x, s[1] + m * y, s[2] + m * z))
        return tuple(out)

    zero = jnp.zeros((8, LANES), F32)
    sums = lax.fori_loop(0, SUB, step, ((zero,) * 3,) * len(u), unroll=16)
    rows = [zero] * 6
    for one, g in zip(u, sums):
        for c in range(3):
            n, o = (c + 1) % 3, (c + 2) % 3
            rows[c] = rows[c] + g[c]
            rows[3 + c] = rows[3 + c] + (one[n] * g[o] - one[o] * g[n])
    return stack([jnp.sum(t, 0, keepdims=True) for t in rows], 8)


def full_tile(u_ref, w_ref):
    rows = SUB // 4

    def quarter(h, terms):
        u = [[u_ref[c, pl.ds(h * rows + 8 * k, 8), :] for c in range(4)] for k in range(rows // 8)]
        return terms + interact(u, w_ref)

    return lax.fori_loop(0, 4, quarter, jnp.zeros((8, LANES), F32))


def unit(start, width, u_ref, w_ref, v_ref):
    parts = LANES // width
    rows = SUB // parts
    def wanted(count):
        lane = iota((count, LANES), 1)
        return (lane >= start) & (lane < start + width)

    def copied(block):
        block = jnp.where(wanted(SUB), block, 0.0)
        step = width
        while step < LANES:
            block = block + pltpu.roll(block, step, 1)
            step *= 2
        return block

    def dealt(blocks):
        out = jnp.where(wanted(rows), blocks[0], 0.0)
        for h in range(1, parts):
            out = out + pltpu.roll(jnp.where(wanted(rows), blocks[h], 0.0), h * width, 1)
        return pltpu.roll(out, (LANES - start) & (LANES - 1), 1)

    for c in range(4):
        v_ref[c] = copied(w_ref[c])
    mine = [dealt([u_ref[c, h * rows : (h + 1) * rows, :] for h in range(parts)]) for c in range(4)]
    u = [[mine[c][8 * k : 8 * k + 8] for c in range(4)] for k in range(rows // 8)]
    found = interact(u, v_ref)
    step = LANES // 2
    while step >= width:
        found = found + pltpu.roll(found, step, 1)
        step //= 2
    return jnp.where(wanted(8), found, 0.0)


def part_tile(count, u_ref, w_ref, v_ref):
    whole = (count + 15) // 32

    def step(n, terms):
        return terms + unit(n * 32, 32, u_ref, w_ref, v_ref)

    terms = lax.fori_loop(0, whole, step, jnp.zeros((8, LANES), F32))
    return lax.cond(
        count > whole * 32, lambda: terms + unit(whole * 32, 16, u_ref, w_ref, v_ref), lambda: terms
    )


def prepare_kernel(
    position_hbm, velocity_hbm, accel_hbm, turn_hbm, kind_hbm, first_hbm, second_hbm, neck_hbm,
    cross_first_hbm, cross_second_hbm, cross_neck_hbm, export_hbm,
    moved_ref, pose_ref, list_ref, near_ref, far1_ref, far2_ref, far3_ref,
    position_ref, velocity_ref, accel_ref, turn_ref, kind_ref, first_ref, second_ref, neck_ref,
    cross_first_ref, cross_second_ref, cross_neck_ref, export_ref, sems,
):
    sources = (
        position_hbm, velocity_hbm, accel_hbm, turn_hbm, kind_hbm, first_hbm, second_hbm, neck_hbm,
        cross_first_hbm, cross_second_hbm, cross_neck_hbm, export_hbm,
    )
    targets = (
        position_ref, velocity_ref, accel_ref, turn_ref, kind_ref, first_ref, second_ref, neck_ref,
        cross_first_ref, cross_second_ref, cross_neck_ref, export_ref,
    )
    copies = [pltpu.make_async_copy(a, b, sems.at[k]) for k, (a, b) in enumerate(zip(sources, targets))]
    for copy in copies:
        copy.start()
    for copy in copies:
        copy.wait()
    group = lax.axis_index("group")
    moved = position_ref[...] + time_step * velocity_ref[...] + 0.5 * time_step**2 * accel_ref[...]
    moved_ref[...] = moved
    pose_ref[0:3, :] = moved
    pose_ref[3:12, :] = turn_ref[...]
    pose_ref[12:13, :] = kind_ref[...].astype(F32)
    pose_ref[13:16, :] = jnp.zeros((3, GRAINS_DEV), F32)
    index = jnp.concatenate([first_ref[...], wide(cross_first_ref[...]), export_ref[...]], 1)
    got = joined(dot(thirds(pose_ref[...]), hot(index, GRAINS_DEV)))
    at = iota((16, LANES), 0)
    second, neck = second_ref[...].astype(F32), neck_ref[...]
    cross_second, cross_neck = wide(cross_second_ref[...]).astype(F32), wide(cross_neck_ref[...])
    near_ref[0:16, :] = pose_ref[:, :BOUND_DEV]
    near_ref[16:32, :] = jnp.where(at == 14, neck, jnp.where(at == 13, second, got[:, :LANES]))
    listed = jnp.where(at == 14, cross_neck, jnp.where(at == 13, cross_second, got[:, LANES : 2 * LANES]))
    exported = got[:, 2 * LANES :]
    for k, far_ref in ((1, far1_ref), (2, far2_ref), (3, far3_ref)):
        to = (group + k) & 3
        turned = pltpu.roll(exported, (64 - CX * to) & (LANES - 1), 1)
        far_ref[...] = jnp.where(iota((16, LANES), 1) < 64, listed, turned)
    first, cross_first = first_ref[...].astype(F32), wide(cross_first_ref[...]).astype(F32)
    list_ref[...] = stack(
        [first, second, neck, cross_first, cross_second, cross_neck, export_ref[...].astype(F32)], 8
    )


def tiles(total, ranks, parts, other_of, poses_ref, table_ref, out_ref, work, both):
    u_ref, w_ref, v_ref, terms_ref = work

    def tile(t, carry):
        fields = picked(ranks, parts, t * WIDTH)
        own = hot(fields[0:1].astype(I32) - 1, GRAINS_DEV)
        mine = joined(dot(poses_ref[...], own))
        other = hot(fields[1:2].astype(I32) - 1, other_of.shape[1])
        theirs = joined(dot(other_of[...], other))
        shift = [SCALE * (mine[c : c + 1] - theirs[c : c + 1]) for c in range(3)]
        second = worlds(table_ref, theirs)
        first = worlds(table_ref, mine)
        first = [first[c] + shift[c] for c in range(3)] + [first[3] - BOND * fields[2:3]]
        for n in range(HALVES):
            for c in range(4):
                w_ref[n, c] = second[c][:, n * LANES : (n + 1) * LANES]
                u_ref[n, c] = first[c][:, n * LANES : (n + 1) * LANES]
        terms_ref[...] = jnp.zeros_like(terms_ref)
        left = total - t * WIDTH

        def half(n, none):
            count = jnp.minimum(left - n * LANES, LANES)
            terms_ref[n] = lax.cond(
                count > 96,
                lambda: full_tile(u_ref.at[n], w_ref.at[n]),
                lambda: part_tile(count, u_ref.at[n], w_ref.at[n], v_ref),
            )
            return none

        lax.fori_loop(0, jnp.minimum(HALVES, (left + LANES - 1) // LANES), half, 0)
        terms = jnp.concatenate([terms_ref[n] for n in range(HALVES)], 1)
        force = [terms[c : c + 1] for c in range(3)]
        rows = [f * (1 / SCALE) for f in force]
        for c in range(3):
            n, o = (c + 1) % 3, (c + 2) % 3
            rows.append((terms[3 + c : 4 + c] - (shift[n] * force[o] - shift[o] * force[n])) * (1 / SCALE**2))
        found = joined(dot_t(thirds(stack(rows, 8)), own))
        if both:
            back = [-r for r in rows[:3]] + [terms[3 + c : 4 + c] * (-1 / SCALE**2) for c in range(3)]
            found = found + joined(dot_t(thirds(stack(back, 8)), other))
        out_ref[...] += found
        return carry

    lax.fori_loop(0, (total + WIDTH - 1) // WIDTH, tile, 0)


def listed(list_ref):
    rows = [list_ref[k : k + 1, :] for k in range(7)]
    return [row if k in (2, 5, 6) else row.astype(I32) for k, row in enumerate(rows)]


def local_kernel(
    poses_in_ref, list_ref, offset_ref, radius_ref,
    out_ref, table_ref,
    poses_ref, *work,
):
    group = lax.axis_index("group")
    blank = jnp.zeros((LANES - KINDS, SUB), F32)
    for e in range(4):
        rows = radius_ref[...] if e == 3 else offset_ref[:, e, :]
        hi = rows.astype(BF16).astype(F32)
        mid = (rows - hi).astype(BF16).astype(F32)
        low = rows - hi - mid
        table_ref[e * SUB : (e + 1) * SUB, :LANES] = jnp.concatenate([hi, mid], 0).T.astype(BF16)
        table_ref[e * SUB : (e + 1) * SUB, LANES:] = jnp.concatenate([low, blank], 0).T.astype(BF16)
    poses_ref[...] = thirds(poses_in_ref[...])
    out_ref[...] = jnp.zeros_like(out_ref)
    first, second, neck, cross_first, cross, cross_neck, export = listed(list_ref)
    ours = (cross >> 5 == group) & (iota((1, LANES), 1) < 64)
    slot = joined(dot(thirds(stack([export], 16)), hot(cross, LANES)))[0:1]
    partner = (first + 1 + second) & (GRAINS_DEV - 1)
    ranks, parts, total = compact(
        [second < GRAINS_DEV - 1, ours],
        [
            [(first + 1).astype(F32), (partner + 1).astype(F32), neck],
            [(cross_first + 1).astype(F32), slot + 1, cross_neck],
        ],
    )
    tiles(total, ranks, parts, poses_ref, poses_ref, table_ref, out_ref, work, True)


def remote_kernel(
    poses_in_ref, list_ref, table_ref, local_ref, velocity_ref, accel_ref, spin_ref, before_ref, after_ref, far1_ref, far2_ref, far3_ref,
    velocity_out_ref, spin_out_ref,
    poses_ref, pool_ref, out_ref, *work,
):
    group = lax.axis_index("group")
    lane = iota((1, LANES), 1)
    poses_ref[...] = thirds(poses_in_ref[...])
    fars = (far1_ref, far2_ref, far3_ref)
    pool = [before_ref[0:16, :], after_ref[0:16, :], before_ref[16:32, :], after_ref[16:32, :]]
    pool_ref[...] = thirds(jnp.concatenate(pool + [f[...] for f in fars], 1))
    out_ref[...] = local_ref[...]
    actives, fields = [], []

    def add(active, own, place, neck):
        actives.append(active)
        fields.append([(own + 1).astype(F32), (place + 1).astype(F32), neck])

    first, second, neck, cross_first, cross, cross_neck, export = listed(list_ref)
    beyond = second - (GRAINS_DEV - 1)
    add(beyond >= 0, first, beyond, neck)
    way = (group - (cross >> 5)) & 3
    add(
        (way != 0) & (lane < 64),
        cross_first,
        3 * LANES + way * LANES + 64 + (cross & (CX - 1)),
        cross_neck,
    )
    beyond = before_ref[29:30, :].astype(I32) - (GRAINS_DEV - 1)
    add(beyond >= BOUND_DEV, beyond - BOUND_DEV, 2 * LANES + lane, before_ref[30:31, :])
    beyond = after_ref[29:30, :].astype(I32) - (GRAINS_DEV - 1)
    add((beyond >= 0) & (beyond < BOUND_DEV), beyond, 3 * LANES + lane, after_ref[30:31, :])
    exports = thirds(stack([export], 16))
    for k in (1, 2, 3):
        wanted = fars[k - 1][13:14, :].astype(I32)
        sender = (group - k) & 3
        slot = joined(dot(exports, hot(sender * CX + (wanted & (CX - 1)), LANES)))[0:1]
        add(
            (wanted >> 5 == group) & (lane < 64),
            slot,
            (3 + k) * LANES + lane,
            fars[k - 1][14:15, :],
        )
    ranks, parts, total = compact(actives, fields)
    tiles(total, ranks, parts, pool_ref, poses_ref, table_ref, out_ref, work, False)
    velocity_out_ref[...] = velocity_ref[...] + 0.5 * time_step * (accel_ref[...] + out_ref[0:3, :])
    spin_out_ref[...] = spin_ref[...] + time_step * out_ref[3:6, :] / inertia


def shifted(array, axis, by):
    devices = lax.axis_size(axis)
    return lax.ppermute(array, axis, [(i, (i + by) % devices) for i in range(devices)])


def shape(rows, columns, kind=F32):
    return jax.ShapeDtypeStruct((rows, columns), kind)


def on_device(
    position, velocity, accel_old, orientation, spin, shape_index, shape_offsets, shape_radii,
    pair_first, pair_second, pair_neck, cross_first, cross_second, cross_neck, export_slots,
):
    row = lambda x: x.reshape(1, x.shape[0])
    sources = (position, velocity, accel_old, orientation) + tuple(
        row(x)
        for x in (
            shape_index, pair_first, pair_second, pair_neck, cross_first, cross_second, cross_neck, export_slots
        )
    )
    moved, poses, lists, near, far1, far2, far3 = pl.pallas_call(
        prepare_kernel,
        in_specs=[pl.BlockSpec(memory_space=pltpu.MemorySpace.HBM)] * 12,
        out_shape=(
            shape(3, GRAINS_DEV), shape(16, GRAINS_DEV), shape(8, LANES), shape(32, LANES),
            shape(16, LANES), shape(16, LANES), shape(16, LANES),
        ),
        scratch_shapes=[pltpu.VMEM(x.shape, x.dtype) for x in sources] + [pltpu.SemaphoreType.DMA((12,))],
        compiler_params=pltpu.CompilerParams(vmem_limit_bytes=60 << 20),
        name="prepare",
    )(*sources)
    before = shifted(near, "region", 1)
    after = shifted(near, "region", -1)
    fars = [shifted(f, "group", k) for k, f in ((1, far1), (2, far2), (3, far3))]
    work = [
        pltpu.VMEM((HALVES, 4, SUB, LANES), F32),
        pltpu.VMEM((HALVES, 4, SUB, LANES), F32),
        pltpu.VMEM((4, SUB, LANES), F32),
        pltpu.VMEM((HALVES, 8, LANES), F32),
    ]
    local, table = pl.pallas_call(
        local_kernel,
        out_shape=(shape(8, GRAINS_DEV), shape(4 * SUB, 4 * KINDS, BF16)),
        scratch_shapes=[pltpu.VMEM((48, GRAINS_DEV), BF16)] + work,
        compiler_params=pltpu.CompilerParams(vmem_limit_bytes=32 << 20),
        cost_estimate=pl.CostEstimate(flops=4_000_000_000, bytes_accessed=1_000_000, transcendentals=4_000_000),
        name="local",
    )(poses, lists, shape_offsets, shape_radii)
    velocity_new, spin_new = pl.pallas_call(
        remote_kernel,
        out_shape=(shape(3, GRAINS_DEV), shape(3, GRAINS_DEV)),
        scratch_shapes=[
            pltpu.VMEM((48, GRAINS_DEV), BF16), pltpu.VMEM((48, 7 * LANES), BF16), pltpu.VMEM((8, GRAINS_DEV), F32)
        ] + work,
        compiler_params=pltpu.CompilerParams(vmem_limit_bytes=32 << 20),
        name="remote",
    )(poses, lists, table, local, velocity, accel_old, spin, before, after, *fars)
    return (moved, velocity_new, spin_new)


def solution(mesh):
    both = ("group", "region")
    wide_spec, flat = P(None, both), P(both)
    return jax.shard_map(
        on_device,
        mesh=mesh,
        in_specs=(wide_spec,) * 5 + (flat, P(), P()) + (flat,) * 7,
        out_specs=(wide_spec,) * 3,
        check_vma=False,
    )
```

profile of v0, /device:TPU:8, one launch (start us, length us, event | category | flops | bytes accessed | tf_op | source)
XLA Modules:
  0.0 33.7 jit_solution(17779136894119794155)
XLA Ops:
  0.6 0.0 copy-start.6
  0.6 2.0 %prepare.1 = (f32[3,1024]{1,0:T(4,128)}, f32[16,1024]{1,0:T(8,128)}, f32[8,128]{1,0:T(8,128)}, f32[32,128]{1,0:T(8,128)}, f32[16,128]{1,0:T(8,128)}, /*index=5*/f32[16,128]{1,0:T(8,128)}, f32[16,128]{1,0:T(8,128)}) custom-call(f32[3,1024]{1,0:T(4,128)} %position_hbm.1, f32[3,1024]{1,0:T(4,128)} %velocity_ref.1, f32[3,1024]{1,0:T(4,128)} %accel_ref.1, ...), custom_call_target="tpu_custom_call" | custom-call | tf_op jit(solution)/shard_map/prepare/pallas_call | solution.py:383
  2.6 0.1 collective-permute-start
  2.7 7.6 %collective-permute-start.1 = (f32[32,128]{1,0:T(8,128)}, f32[32,128]{1,0:T(8,128)S(1)}, u32[]{:S(2)}, u32[]{:S(2)}) collective-permute-start(f32[32,128]{1,0:T(8,128)} %get-tuple-element.19), channel_id=1, source_target_pairs={{0,63},{1,0},{2,1},{3,2},{4,3},{5,4},{6,5},{7,6},{8,7},{9,8},{10,9... | collective-permute-start | bytes 49160 | tf_op jit(solution)/shard_map/ppermute | solution.py:365
  10.3 1.6 %collective-permute-start.2 = (f32[16,128]{1,0:T(8,128)}, f32[16,128]{1,0:T(8,128)S(1)}, u32[]{:S(2)}, u32[]{:S(2)}) collective-permute-start(f32[16,128]{1,0:T(8,128)} %get-tuple-element.20), channel_id=1, source_target_pairs={{0,64},{64,128},{128,192},{192,0},{1,65},{65,129},{129,193},{193,1... | collective-permute-start | bytes 24584 | tf_op jit(solution)/shard_map/ppermute | solution.py:365
  11.9 0.9 %collective-permute-start.3 = (f32[16,128]{1,0:T(8,128)}, f32[16,128]{1,0:T(8,128)S(1)}, u32[]{:S(2)}, u32[]{:S(2)}) collective-permute-start(f32[16,128]{1,0:T(8,128)} %get-tuple-element.21), channel_id=1, source_target_pairs={{0,128},{64,192},{128,0},{192,64},{1,129},{65,193},{129,1},{193,65... | collective-permute-start | bytes 24584 | tf_op jit(solution)/shard_map/ppermute | solution.py:365
  12.8 0.0 copy-start
  12.8 0.0 copy-start.4
  12.8 0.0 copy-start.5
  12.8 2.4 %collective-permute-start.4 = (f32[16,128]{1,0:T(8,128)}, f32[16,128]{1,0:T(8,128)S(1)}, u32[]{:S(2)}, u32[]{:S(2)}) collective-permute-start(f32[16,128]{1,0:T(8,128)} %get-tuple-element.22), channel_id=1, source_target_pairs={{0,192},{64,0},{128,64},{192,128},{1,193},{65,1},{129,65},{193,129... | collective-permute-start | bytes 24584 | tf_op jit(solution)/shard_map/ppermute | solution.py:365
  15.2 0.0 copy-done.6
  15.2 0.1 copy.18.offset_ref
  15.3 0.0 copy-done
  15.3 0.0 copy-done.4
  15.3 0.0 copy-done.5
  15.3 0.0 copy-start.1
  15.4 0.0 copy-start.2
  15.4 0.0 copy-start.3
  15.4 8.1 %local.1 = (f32[8,1024]{1,0:T(8,128)S(1)}, bf16[512,256]{1,0:T(8,128)(2,1)S(1)}) custom-call(f32[16,1024]{1,0:T(8,128)S(1)} %copy-done, f32[8,128]{1,0:T(8,128)S(1)} %copy-done.4, f32[64,3,128]{2,1,0:T(4,128)S(1)} %copy.18.offset_ref, f32[64,128]{1,0:T(8,128)S(1)} %copy-done.5), custom_call_target="tpu_custom_call" | custom-call | flops 4000000000 | bytes 1000000 | tf_op jit(solution)/shard_map/local/pallas_call | solution.py:403
  23.5 0.0 collective-permute-done.2.far1_ref
  23.5 0.0 collective-permute-done.3.far2_ref
  23.5 0.0 collective-permute-done.4.far3_ref
  23.5 0.0 collective-permute-done.before_ref
  23.5 0.0 collective-permute-done.1.after_ref
  23.5 0.0 copy-done.1
  23.6 0.0 copy-done.2
  23.6 0.0 copy-done.3
  23.6 10.1 %remote.1 = (f32[3,1024]{1,0:T(4,128)}, f32[3,1024]{1,0:T(4,128)}) custom-call(f32[16,1024]{1,0:T(8,128)S(1)} %copy-done, f32[8,128]{1,0:T(8,128)S(1)} %copy-done.4, bf16[512,256]{1,0:T(8,128)(2,1)S(1)} %get-tuple-element.17.table_ref, f32[8,1024]{1,0:T(8,128)S(1)} %get-tuple-element.18.local_ref, f32[3,1024]{1,0:T(4,128)S(1)} %copy-done.1, ...), custom_call_target="tpu_custom_call" | custom-call | tf_op jit(solution)/shard_map/remote/pallas_call | solution.py:411
Async XLA Ops:
  0.6 14.6 %copy-start.6 = (f32[64,3,128]{2,0,1:T(8,128)S(1)}, f32[64,3,128]{2,0,1:T(8,128)}, u32[]{:S(2)}) copy-start(f32[64,3,128]{2,0,1:T(8,128)} %param.21) | copy-start | bytes 294916
  2.6 20.9 %collective-permute-start = (f32[32,128]{1,0:T(8,128)}, f32[32,128]{1,0:T(8,128)S(1)}, u32[]{:S(2)}, u32[]{:S(2)}) collective-permute-start(f32[32,128]{1,0:T(8,128)} %get-tuple-element.19), channel_id=1, source_target_pairs={{0,1},{1,2},{2,3},{3,4},{4,5},{5,6},{6,7},{7,8},{8,9},{9,10},{10,1... | collective-permute-start | bytes 49160 | tf_op jit(solution)/shard_map/ppermute | solution.py:365
  2.7 20.8 %collective-permute-start.1 = (f32[32,128]{1,0:T(8,128)}, f32[32,128]{1,0:T(8,128)S(1)}, u32[]{:S(2)}, u32[]{:S(2)}) collective-permute-start(f32[32,128]{1,0:T(8,128)} %get-tuple-element.19), channel_id=1, source_target_pairs={{0,63},{1,0},{2,1},{3,2},{4,3},{5,4},{6,5},{7,6},{8,7},{9,8},{10,9... | collective-permute-start | bytes 49160 | tf_op jit(solution)/shard_map/ppermute | solution.py:365
  10.3 13.2 %collective-permute-start.2 = (f32[16,128]{1,0:T(8,128)}, f32[16,128]{1,0:T(8,128)S(1)}, u32[]{:S(2)}, u32[]{:S(2)}) collective-permute-start(f32[16,128]{1,0:T(8,128)} %get-tuple-element.20), channel_id=1, source_target_pairs={{0,64},{64,128},{128,192},{192,0},{1,65},{65,129},{129,193},{193,1... | collective-permute-start | bytes 24584 | tf_op jit(solution)/shard_map/ppermute | solution.py:365
  11.9 11.6 %collective-permute-start.3 = (f32[16,128]{1,0:T(8,128)}, f32[16,128]{1,0:T(8,128)S(1)}, u32[]{:S(2)}, u32[]{:S(2)}) collective-permute-start(f32[16,128]{1,0:T(8,128)} %get-tuple-element.21), channel_id=1, source_target_pairs={{0,128},{64,192},{128,0},{192,64},{1,129},{65,193},{129,1},{193,65... | collective-permute-start | bytes 24584 | tf_op jit(solution)/shard_map/ppermute | solution.py:365
  12.8 2.5 %copy-start = (f32[16,1024]{1,0:T(8,128)S(1)}, f32[16,1024]{1,0:T(8,128)}, u32[]{:S(2)}) copy-start(f32[16,1024]{1,0:T(8,128)} %get-tuple-element.15.poses_in_ref) | copy-start | bytes 196612
  12.8 2.5 %copy-start.4 = (f32[8,128]{1,0:T(8,128)S(1)}, f32[8,128]{1,0:T(8,128)}, u32[]{:S(2)}) copy-start(f32[8,128]{1,0:T(8,128)} %get-tuple-element.16.list_ref) | copy-start | bytes 12292
  12.8 2.5 %copy-start.5 = (f32[64,128]{1,0:T(8,128)S(1)}, f32[64,128]{1,0:T(8,128)}, u32[]{:S(2)}) copy-start(f32[64,128]{1,0:T(8,128)} %radius_ref.1) | copy-start | bytes 98308
  12.8 10.7 %collective-permute-start.4 = (f32[16,128]{1,0:T(8,128)}, f32[16,128]{1,0:T(8,128)S(1)}, u32[]{:S(2)}, u32[]{:S(2)}) collective-permute-start(f32[16,128]{1,0:T(8,128)} %get-tuple-element.22), channel_id=1, source_target_pairs={{0,192},{64,0},{128,64},{192,128},{1,193},{65,1},{129,65},{193,129... | collective-permute-start | bytes 24584 | tf_op jit(solution)/shard_map/ppermute | solution.py:365
  15.3 8.2 %copy-start.1 = (f32[3,1024]{1,0:T(4,128)S(1)}, f32[3,1024]{1,0:T(4,128)}, u32[]{:S(2)}) copy-start(f32[3,1024]{1,0:T(4,128)} %velocity_ref.1) | copy-start | bytes 36868
  15.4 8.2 %copy-start.2 = (f32[3,1024]{1,0:T(4,128)S(1)}, f32[3,1024]{1,0:T(4,128)}, u32[]{:S(2)}) copy-start(f32[3,1024]{1,0:T(4,128)} %accel_ref.1) | copy-start | bytes 36868
  15.4 8.2 %copy-start.3 = (f32[3,1024]{1,0:T(4,128)S(1)}, f32[3,1024]{1,0:T(4,128)}, u32[]{:S(2)}) copy-start(f32[3,1024]{1,0:T(4,128)} %spin_ref.1) | copy-start | bytes 36868
where the time goes:
time: 34 us; the launch traced here: 33.7 us
  Pallas kernels  20.2 us (59%)
  starting transfers between devices  12.6 us (37%)
  between operations  0.78 us (2%)
    ppermute x5, starting transfers between devices, shifted(): lax.ppermute(array, axis, [(i, (i + by) % devices) for i in range(devices)])  12.6 us
    pallas_call x1, Pallas kernels, on_device(): pl.pallas_call(remote_kernel, out_shape=(shape(3, GRAINS_DEV), shape(3, G...  10.1 us
    pallas_call x1, Pallas kernels, on_device(): pl.pallas_call(local_kernel, out_shape=(shape(8, GRAINS_DEV), shape(4 * S...  8.09 us
    pallas_call x1, Pallas kernels, on_device(): pl.pallas_call(prepare_kernel, in_specs=[pl.BlockSpec(memory_space=pltpu....  1.99 us
  transfers between devices with their start and end apart: 5, of which 0 were waited for; matrix products, arithmetic and copies ran while one was open for 0% of the time, Pallas kernels for 24%

commit v1 on v0

--- a/solution.py
+++ b/solution.py
@@ -90,8 +90,9 @@
     return jnp.concatenate(ranks, 1), parts, total
 
 
-def picked(ranks, parts, base):
-    want = iota((WIDTH, ranks.shape[1]), 0) + base
+def picked(ranks, parts, base, widths):
+    at = iota((WIDTH, ranks.shape[1]), 0)
+    want = base + jnp.where(at < LANES, at & (widths[0] - 1), LANES + (at & (widths[1] - 1)))
     chosen = jnp.where(want == ranks, 1.0, 0.0).astype(BF16)
     return joined(dot_t(parts, chosen))
 
@@ -126,70 +127,43 @@
             n, o = (c + 1) % 3, (c + 2) % 3
             rows[c] = rows[c] + g[c]
             rows[3 + c] = rows[3 + c] + (one[n] * g[o] - one[o] * g[n])
-    return stack([jnp.sum(t, 0, keepdims=True) for t in rows], 8)
-
-
-def full_tile(u_ref, w_ref):
-    rows = SUB // 4
-
-    def quarter(h, terms):
-        u = [[u_ref[c, pl.ds(h * rows + 8 * k, 8), :] for c in range(4)] for k in range(rows // 8)]
-        return terms + interact(u, w_ref)
-
-    return lax.fori_loop(0, 4, quarter, jnp.zeros((8, LANES), F32))
-
-
-def unit(start, width, u_ref, w_ref, v_ref):
-    parts = LANES // width
-    rows = SUB // parts
-    def wanted(count):
-        lane = iota((count, LANES), 1)
-        return (lane >= start) & (lane < start + width)
-
-    def copied(block):
-        block = jnp.where(wanted(SUB), block, 0.0)
-        step = width
-        while step < LANES:
-            block = block + pltpu.roll(block, step, 1)
-            step *= 2
-        return block
-
-    def dealt(blocks):
-        out = jnp.where(wanted(rows), blocks[0], 0.0)
-        for h in range(1, parts):
-            out = out + pltpu.roll(jnp.where(wanted(rows), blocks[h], 0.0), h * width, 1)
-        return pltpu.roll(out, (LANES - start) & (LANES - 1), 1)
-
+    return rows
+
+
+def dealt(u_ref, width):
+    rows = SUB * width // LANES
+    part = iota((rows, LANES), 1) // width
     for c in range(4):
-        v_ref[c] = copied(w_ref[c])
-    mine = [dealt([u_ref[c, h * rows : (h + 1) * rows, :] for h in range(parts)]) for c in range(4)]
-    u = [[mine[c][8 * k : 8 * k + 8] for c in range(4)] for k in range(rows // 8)]
-    found = interact(u, v_ref)
-    step = LANES // 2
-    while step >= width:
-        found = found + pltpu.roll(found, step, 1)
-        step //= 2
-    return jnp.where(wanted(8), found, 0.0)
-
-
-def part_tile(count, u_ref, w_ref, v_ref):
-    whole = (count + 15) // 32
-
-    def step(n, terms):
-        return terms + unit(n * 32, 32, u_ref, w_ref, v_ref)
-
-    terms = lax.fori_loop(0, whole, step, jnp.zeros((8, LANES), F32))
-    return lax.cond(
-        count > whole * 32, lambda: terms + unit(whole * 32, 16, u_ref, w_ref, v_ref), lambda: terms
-    )
+        value = u_ref[c, :rows, :]
+        for h in range(1, LANES // width):
+            value = jnp.where(part == h, u_ref[c, h * rows : (h + 1) * rows, :], value)
+        u_ref[c, :rows, :] = value
+
+
+def half_tile(width, u_ref, w_ref):
+    def blocks(h, count):
+        return [[u_ref[c, pl.ds(h * 32 + 8 * k, 8), :] for c in range(4)] for k in range(count)]
+
+    for size in (64, 32, 16):
+        pl.when(width == size)(functools.partial(dealt, u_ref, size))
+    zero = (jnp.zeros((8, LANES), F32),) * 6
+
+    def whole():
+        def step(h, terms):
+            return tuple(a + b for a, b in zip(terms, interact(blocks(h, 4), w_ref)))
+
+        return lax.fori_loop(0, width // 32, step, zero)
+
+    terms = lax.cond(width == 16, lambda: tuple(interact(blocks(0, 2), w_ref)), whole)
+    return stack([jnp.sum(t, 0, keepdims=True) for t in terms], 8)
 
 
 def prepare_kernel(
     position_hbm, velocity_hbm, accel_hbm, turn_hbm, kind_hbm, first_hbm, second_hbm, neck_hbm,
     cross_first_hbm, cross_second_hbm, cross_neck_hbm, export_hbm,
-    moved_ref, pose_ref, list_ref, near_ref, far1_ref, far2_ref, far3_ref,
+    moved_ref, thirds_ref, list_ref, near_ref, far1_ref, far2_ref, far3_ref,
     position_ref, velocity_ref, accel_ref, turn_ref, kind_ref, first_ref, second_ref, neck_ref,
-    cross_first_ref, cross_second_ref, cross_neck_ref, export_ref, sems,
+    cross_first_ref, cross_second_ref, cross_neck_ref, export_ref, pose_ref, sems,
 ):
     sources = (
         position_hbm, velocity_hbm, accel_hbm, turn_hbm, kind_hbm, first_hbm, second_hbm, neck_hbm,
@@ -212,7 +186,9 @@
     pose_ref[12:13, :] = kind_ref[...].astype(F32)
     pose_ref[13:16, :] = jnp.zeros((3, GRAINS_DEV), F32)
     index = jnp.concatenate([first_ref[...], wide(cross_first_ref[...]), export_ref[...]], 1)
-    got = joined(dot(thirds(pose_ref[...]), hot(index, GRAINS_DEV)))
+    poses = thirds(pose_ref[...])
+    thirds_ref[...] = poses
+    got = joined(dot(poses, hot(index, GRAINS_DEV)))
     at = iota((16, LANES), 0)
     second, neck = second_ref[...].astype(F32), neck_ref[...]
     cross_second, cross_neck = wide(cross_second_ref[...]).astype(F32), wide(cross_neck_ref[...])
@@ -231,10 +207,15 @@
 
 
 def tiles(total, ranks, parts, other_of, poses_ref, table_ref, out_ref, work, both):
-    u_ref, w_ref, v_ref, terms_ref = work
+    u_ref, w_ref, terms_ref = work
 
     def tile(t, carry):
-        fields = picked(ranks, parts, t * WIDTH)
+        left = total - t * WIDTH
+        counts = [left - n * LANES for n in range(HALVES)]
+        widths = [
+            jnp.where(n <= 16, 16, jnp.where(n <= 32, 32, jnp.where(n <= 64, 64, LANES))).astype(I32) for n in counts
+        ]
+        fields = picked(ranks, parts, t * WIDTH, widths)
         own = hot(fields[0:1].astype(I32) - 1, GRAINS_DEV)
         mine = joined(dot(poses_ref[...], own))
         other = hot(fields[1:2].astype(I32) - 1, other_of.shape[1])
@@ -248,15 +229,10 @@
                 w_ref[n, c] = second[c][:, n * LANES : (n + 1) * LANES]
                 u_ref[n, c] = first[c][:, n * LANES : (n + 1) * LANES]
         terms_ref[...] = jnp.zeros_like(terms_ref)
-        left = total - t * WIDTH
 
         def half(n, none):
-            count = jnp.minimum(left - n * LANES, LANES)
-            terms_ref[n] = lax.cond(
-                count > 96,
-                lambda: full_tile(u_ref.at[n], w_ref.at[n]),
-                lambda: part_tile(count, u_ref.at[n], w_ref.at[n], v_ref),
-            )
+            width = jnp.where(n == 0, widths[0], widths[1])
+            terms_ref[n] = half_tile(width, u_ref.at[n], w_ref.at[n])
             return none
 
         lax.fori_loop(0, jnp.minimum(HALVES, (left + LANES - 1) // LANES), half, 0)
@@ -282,9 +258,9 @@
 
 
 def local_kernel(
-    poses_in_ref, list_ref, offset_ref, radius_ref,
+    poses_ref, list_ref, offset_ref, radius_ref,
     out_ref, table_ref,
-    poses_ref, *work,
+    *work,
 ):
     group = lax.axis_index("group")
     blank = jnp.zeros((LANES - KINDS, SUB), F32)
@@ -295,7 +271,6 @@
         low = rows - hi - mid
         table_ref[e * SUB : (e + 1) * SUB, :LANES] = jnp.concatenate([hi, mid], 0).T.astype(BF16)
         table_ref[e * SUB : (e + 1) * SUB, LANES:] = jnp.concatenate([low, blank], 0).T.astype(BF16)
-    poses_ref[...] = thirds(poses_in_ref[...])
     out_ref[...] = jnp.zeros_like(out_ref)
     first, second, neck, cross_first, cross, cross_neck, export = listed(list_ref)
     ours = (cross >> 5 == group) & (iota((1, LANES), 1) < 64)
@@ -312,13 +287,12 @@
 
 
 def remote_kernel(
-    poses_in_ref, list_ref, table_ref, local_ref, velocity_ref, accel_ref, spin_ref, before_ref, after_ref, far1_ref, far2_ref, far3_ref,
+    poses_ref, list_ref, table_ref, local_ref, velocity_ref, accel_ref, spin_ref, before_ref, after_ref, far1_ref, far2_ref, far3_ref,
     velocity_out_ref, spin_out_ref,
-    poses_ref, pool_ref, out_ref, *work,
+    pool_ref, out_ref, *work,
 ):
     group = lax.axis_index("group")
     lane = iota((1, LANES), 1)
-    poses_ref[...] = thirds(poses_in_ref[...])
     fars = (far1_ref, far2_ref, far3_ref)
     pool = [before_ref[0:16, :], after_ref[0:16, :], before_ref[16:32, :], after_ref[16:32, :]]
     pool_ref[...] = thirds(jnp.concatenate(pool + [f[...] for f in fars], 1))
@@ -384,10 +358,11 @@
         prepare_kernel,
         in_specs=[pl.BlockSpec(memory_space=pltpu.MemorySpace.HBM)] * 12,
         out_shape=(
-            shape(3, GRAINS_DEV), shape(16, GRAINS_DEV), shape(8, LANES), shape(32, LANES),
+            shape(3, GRAINS_DEV), shape(48, GRAINS_DEV, BF16), shape(8, LANES), shape(32, LANES),
             shape(16, LANES), shape(16, LANES), shape(16, LANES),
         ),
-        scratch_shapes=[pltpu.VMEM(x.shape, x.dtype) for x in sources] + [pltpu.SemaphoreType.DMA((12,))],
+        scratch_shapes=[pltpu.VMEM(x.shape, x.dtype) for x in sources]
+        + [pltpu.VMEM((16, GRAINS_DEV), F32), pltpu.SemaphoreType.DMA((12,))],
         compiler_params=pltpu.CompilerParams(vmem_limit_bytes=60 << 20),
         name="prepare",
     )(*sources)
@@ -397,13 +372,12 @@
     work = [
         pltpu.VMEM((HALVES, 4, SUB, LANES), F32),
         pltpu.VMEM((HALVES, 4, SUB, LANES), F32),
-        pltpu.VMEM((4, SUB, LANES), F32),
         pltpu.VMEM((HALVES, 8, LANES), F32),
     ]
     local, table = pl.pallas_call(
         local_kernel,
         out_shape=(shape(8, GRAINS_DEV), shape(4 * SUB, 4 * KINDS, BF16)),
-        scratch_shapes=[pltpu.VMEM((48, GRAINS_DEV), BF16)] + work,
+        scratch_shapes=work,
         compiler_params=pltpu.CompilerParams(vmem_limit_bytes=32 << 20),
         cost_estimate=pl.CostEstimate(flops=4_000_000_000, bytes_accessed=1_000_000, transcendentals=4_000_000),
         name="local",
@@ -412,7 +386,7 @@
         remote_kernel,
         out_shape=(shape(3, GRAINS_DEV), shape(3, GRAINS_DEV)),
         scratch_shapes=[
-            pltpu.VMEM((48, GRAINS_DEV), BF16), pltpu.VMEM((48, 7 * LANES), BF16), pltpu.VMEM((8, GRAINS_DEV), F32)
+            pltpu.VMEM((48, 7 * LANES), BF16), pltpu.VMEM((8, GRAINS_DEV), F32)
         ] + work,
         compiler_params=pltpu.CompilerParams(vmem_limit_bytes=32 << 20),
         name="remote",

time: 34 us -> 33.5 us (0.985); the launches traced: 33.7 us -> 33.7 us
  no operation moved by 1% of the time
where the time goes in v1:
time: 33.5 us; the launch traced here: 33.7 us
  Pallas kernels  20.2 us (60%)
  starting transfers between devices  12.6 us (38%)
  between operations  0.78 us (2%)
    ppermute x5, starting transfers between devices, shifted(): lax.ppermute(array, axis, [(i, (i + by) % devices) for i in range(devices)])  12.6 us
    pallas_call x1, Pallas kernels, on_device(): pl.pallas_call(remote_kernel, out_shape=(shape(3, GRAINS_DEV), shape(3, G...  10.1 us
    pallas_call x1, Pallas kernels, on_device(): pl.pallas_call(local_kernel, out_shape=(shape(8, GRAINS_DEV), shape(4 * S...  8.08 us
    pallas_call x1, Pallas kernels, on_device(): pl.pallas_call(prepare_kernel, in_specs=[pl.BlockSpec(memory_space=pltpu....  2 us
  transfers between devices with their start and end apart: 5, of which 0 were waited for; matrix products, arithmetic and copies ran while one was open for 0% of the time, Pallas kernels for 24%

profile of v1, /device:TPU:8, one launch (start us, length us, event | category | flops | bytes accessed | tf_op | source)
XLA Modules:
  0.0 33.7 jit_solution(18032953991261044137)
XLA Ops:
  0.6 0.0 copy-start.6
  0.6 2.0 %prepare.1 = (f32[3,1024]{1,0:T(4,128)}, bf16[48,1024]{1,0:T(8,128)(2,1)}, f32[8,128]{1,0:T(8,128)}, f32[32,128]{1,0:T(8,128)}, f32[16,128]{1,0:T(8,128)}, /*index=5*/f32[16,128]{1,0:T(8,128)}, f32[16,128]{1,0:T(8,128)}) custom-call(f32[3,1024]{1,0:T(4,128)} %position_hbm.1, f32[3,1024]{1,0:T(4,128)} %velocity_ref.1, f32[3,1024]{1,0:T(4,128)} %accel_ref.1, ...), custom_call_target="tpu_custom_call" | custom-call | tf_op jit(solution)/shard_map/prepare/pallas_call | solution.py:357
  2.7 0.1 collective-permute-start
  2.7 7.6 %collective-permute-start.1 = (f32[32,128]{1,0:T(8,128)}, f32[32,128]{1,0:T(8,128)S(1)}, u32[]{:S(2)}, u32[]{:S(2)}) collective-permute-start(f32[32,128]{1,0:T(8,128)} %get-tuple-element.19), channel_id=1, source_target_pairs={{0,63},{1,0},{2,1},{3,2},{4,3},{5,4},{6,5},{7,6},{8,7},{9,8},{10,9... | collective-permute-start | bytes 49160 | tf_op jit(solution)/shard_map/ppermute | solution.py:339
  10.3 1.6 %collective-permute-start.2 = (f32[16,128]{1,0:T(8,128)}, f32[16,128]{1,0:T(8,128)S(1)}, u32[]{:S(2)}, u32[]{:S(2)}) collective-permute-start(f32[16,128]{1,0:T(8,128)} %get-tuple-element.20), channel_id=1, source_target_pairs={{0,64},{64,128},{128,192},{192,0},{1,65},{65,129},{129,193},{193,1... | collective-permute-start | bytes 24584 | tf_op jit(solution)/shard_map/ppermute | solution.py:339
  11.9 0.9 %collective-permute-start.3 = (f32[16,128]{1,0:T(8,128)}, f32[16,128]{1,0:T(8,128)S(1)}, u32[]{:S(2)}, u32[]{:S(2)}) collective-permute-start(f32[16,128]{1,0:T(8,128)} %get-tuple-element.21), channel_id=1, source_target_pairs={{0,128},{64,192},{128,0},{192,64},{1,129},{65,193},{129,1},{193,65... | collective-permute-start | bytes 24584 | tf_op jit(solution)/shard_map/ppermute | solution.py:339
  12.8 0.0 copy-start
  12.8 0.0 copy-start.4
  12.8 0.0 copy-start.5
  12.8 2.4 %collective-permute-start.4 = (f32[16,128]{1,0:T(8,128)}, f32[16,128]{1,0:T(8,128)S(1)}, u32[]{:S(2)}, u32[]{:S(2)}) collective-permute-start(f32[16,128]{1,0:T(8,128)} %get-tuple-element.22), channel_id=1, source_target_pairs={{0,192},{64,0},{128,64},{192,128},{1,193},{65,1},{129,65},{193,129... | collective-permute-start | bytes 24584 | tf_op jit(solution)/shard_map/ppermute | solution.py:339
  15.2 0.0 copy-done.6
  15.2 0.1 copy.18.offset_ref
  15.3 0.0 copy-done
  15.3 0.0 copy-done.4
  15.3 0.0 copy-done.5
  15.4 0.0 copy-start.1
  15.4 0.0 copy-start.2
  15.4 0.0 copy-start.3
  15.4 8.1 %local.1 = (f32[8,1024]{1,0:T(8,128)S(1)}, bf16[512,256]{1,0:T(8,128)(2,1)S(1)}) custom-call(bf16[48,1024]{1,0:T(8,128)(2,1)S(1)} %copy-done, f32[8,128]{1,0:T(8,128)S(1)} %copy-done.4, f32[64,3,128]{2,1,0:T(4,128)S(1)} %copy.18.offset_ref, f32[64,128]{1,0:T(8,128)S(1)} %copy-done.5), custom_call_target="tpu_custom_call" | custom-call | flops 4000000000 | bytes 1000000 | tf_op jit(solution)/shard_map/local/pallas_call | solution.py:377
  23.5 0.0 collective-permute-done.2.far1_ref
  23.5 0.0 collective-permute-done.3.far2_ref
  23.5 0.0 collective-permute-done.4.far3_ref
  23.5 0.0 collective-permute-done.before_ref
  23.5 0.0 collective-permute-done.1.after_ref
  23.5 0.0 copy-done.1
  23.6 0.0 copy-done.2
  23.6 0.0 copy-done.3
  23.6 10.1 %remote.1 = (f32[3,1024]{1,0:T(4,128)}, f32[3,1024]{1,0:T(4,128)}) custom-call(bf16[48,1024]{1,0:T(8,128)(2,1)S(1)} %copy-done, f32[8,128]{1,0:T(8,128)S(1)} %copy-done.4, bf16[512,256]{1,0:T(8,128)(2,1)S(1)} %get-tuple-element.17.table_ref, f32[8,1024]{1,0:T(8,128)S(1)} %get-tuple-element.18.local_ref, f32[3,1024]{1,0:T(4,128)S(1)} %copy-done.1, ...), custom_call_target="tpu_custom_call" | custom-call | tf_op jit(solution)/shard_map/remote/pallas_call | solution.py:385
Async XLA Ops:
  0.6 14.6 %copy-start.6 = (f32[64,3,128]{2,0,1:T(8,128)S(1)}, f32[64,3,128]{2,0,1:T(8,128)}, u32[]{:S(2)}) copy-start(f32[64,3,128]{2,0,1:T(8,128)} %param.21) | copy-start | bytes 294916
  2.7 20.9 %collective-permute-start = (f32[32,128]{1,0:T(8,128)}, f32[32,128]{1,0:T(8,128)S(1)}, u32[]{:S(2)}, u32[]{:S(2)}) collective-permute-start(f32[32,128]{1,0:T(8,128)} %get-tuple-element.19), channel_id=1, source_target_pairs={{0,1},{1,2},{2,3},{3,4},{4,5},{5,6},{6,7},{7,8},{8,9},{9,10},{10,1... | collective-permute-start | bytes 49160 | tf_op jit(solution)/shard_map/ppermute | solution.py:339
  2.7 20.8 %collective-permute-start.1 = (f32[32,128]{1,0:T(8,128)}, f32[32,128]{1,0:T(8,128)S(1)}, u32[]{:S(2)}, u32[]{:S(2)}) collective-permute-start(f32[32,128]{1,0:T(8,128)} %get-tuple-element.19), channel_id=1, source_target_pairs={{0,63},{1,0},{2,1},{3,2},{4,3},{5,4},{6,5},{7,6},{8,7},{9,8},{10,9... | collective-permute-start | bytes 49160 | tf_op jit(solution)/shard_map/ppermute | solution.py:339
  10.3 13.2 %collective-permute-start.2 = (f32[16,128]{1,0:T(8,128)}, f32[16,128]{1,0:T(8,128)S(1)}, u32[]{:S(2)}, u32[]{:S(2)}) collective-permute-start(f32[16,128]{1,0:T(8,128)} %get-tuple-element.20), channel_id=1, source_target_pairs={{0,64},{64,128},{128,192},{192,0},{1,65},{65,129},{129,193},{193,1... | collective-permute-start | bytes 24584 | tf_op jit(solution)/shard_map/ppermute | solution.py:339
  11.9 11.6 %collective-permute-start.3 = (f32[16,128]{1,0:T(8,128)}, f32[16,128]{1,0:T(8,128)S(1)}, u32[]{:S(2)}, u32[]{:S(2)}) collective-permute-start(f32[16,128]{1,0:T(8,128)} %get-tuple-element.21), channel_id=1, source_target_pairs={{0,128},{64,192},{128,0},{192,64},{1,129},{65,193},{129,1},{193,65... | collective-permute-start | bytes 24584 | tf_op jit(solution)/shard_map/ppermute | solution.py:339
  12.8 2.5 %copy-start = (bf16[48,1024]{1,0:T(8,128)(2,1)S(1)}, bf16[48,1024]{1,0:T(8,128)(2,1)}, u32[]{:S(2)}) copy-start(bf16[48,1024]{1,0:T(8,128)(2,1)} %get-tuple-element.15.poses_ref) | copy-start | bytes 294916
  12.8 2.5 %copy-start.4 = (f32[8,128]{1,0:T(8,128)S(1)}, f32[8,128]{1,0:T(8,128)}, u32[]{:S(2)}) copy-start(f32[8,128]{1,0:T(8,128)} %get-tuple-element.16.list_ref) | copy-start | bytes 12292
  12.8 2.5 %copy-start.5 = (f32[64,128]{1,0:T(8,128)S(1)}, f32[64,128]{1,0:T(8,128)}, u32[]{:S(2)}) copy-start(f32[64,128]{1,0:T(8,128)} %radius_ref.1) | copy-start | bytes 98308
  12.8 10.7 %collective-permute-start.4 = (f32[16,128]{1,0:T(8,128)}, f32[16,128]{1,0:T(8,128)S(1)}, u32[]{:S(2)}, u32[]{:S(2)}) collective-permute-start(f32[16,128]{1,0:T(8,128)} %get-tuple-element.22), channel_id=1, source_target_pairs={{0,192},{64,0},{128,64},{192,128},{1,193},{65,1},{129,65},{193,129... | collective-permute-start | bytes 24584 | tf_op jit(solution)/shard_map/ppermute | solution.py:339
  15.4 8.2 %copy-start.1 = (f32[3,1024]{1,0:T(4,128)S(1)}, f32[3,1024]{1,0:T(4,128)}, u32[]{:S(2)}) copy-start(f32[3,1024]{1,0:T(4,128)} %velocity_ref.1) | copy-start | bytes 36868
  15.4 8.2 %copy-start.2 = (f32[3,1024]{1,0:T(4,128)S(1)}, f32[3,1024]{1,0:T(4,128)}, u32[]{:S(2)}) copy-start(f32[3,1024]{1,0:T(4,128)} %accel_ref.1) | copy-start | bytes 36868
  15.4 8.2 %copy-start.3 = (f32[3,1024]{1,0:T(4,128)S(1)}, f32[3,1024]{1,0:T(4,128)}, u32[]{:S(2)}) copy-start(f32[3,1024]{1,0:T(4,128)} %spin_ref.1) | copy-start | bytes 36868

commit v2 on v1

--- a/solution.py
+++ b/solution.py
@@ -120,7 +120,7 @@
         return tuple(out)
 
     zero = jnp.zeros((8, LANES), F32)
-    sums = lax.fori_loop(0, SUB, step, ((zero,) * 3,) * len(u), unroll=16)
+    sums = lax.fori_loop(0, SUB, step, ((zero,) * 3,) * len(u), unroll=32)
     rows = [zero] * 6
     for one, g in zip(u, sums):
         for c in range(3):
@@ -163,7 +163,7 @@
     cross_first_hbm, cross_second_hbm, cross_neck_hbm, export_hbm,
     moved_ref, thirds_ref, list_ref, near_ref, far1_ref, far2_ref, far3_ref,
     position_ref, velocity_ref, accel_ref, turn_ref, kind_ref, first_ref, second_ref, neck_ref,
-    cross_first_ref, cross_second_ref, cross_neck_ref, export_ref, pose_ref, sems,
+    cross_first_ref, cross_second_ref, cross_neck_ref, export_ref, pose_ref, hot_ref, sems,
 ):
     sources = (
         position_hbm, velocity_hbm, accel_hbm, turn_hbm, kind_hbm, first_hbm, second_hbm, neck_hbm,
@@ -174,21 +174,24 @@
         cross_first_ref, cross_second_ref, cross_neck_ref, export_ref,
     )
     copies = [pltpu.make_async_copy(a, b, sems.at[k]) for k, (a, b) in enumerate(zip(sources, targets))]
-    for copy in copies:
-        copy.start()
-    for copy in copies:
-        copy.wait()
+    for k in (5, 8, 11, 3, 0, 1, 2, 4, 6, 7, 9, 10):
+        copies[k].start()
     group = lax.axis_index("group")
+    for k in (5, 8, 11):
+        copies[k].wait()
+    index = jnp.concatenate([first_ref[...], wide(cross_first_ref[...]), export_ref[...]], 1)
+    hot_ref[...] = hot(index, GRAINS_DEV)
+    for k in (3, 0, 1, 2, 4, 6, 7, 9, 10):
+        copies[k].wait()
     moved = position_ref[...] + time_step * velocity_ref[...] + 0.5 * time_step**2 * accel_ref[...]
     moved_ref[...] = moved
     pose_ref[0:3, :] = moved
     pose_ref[3:12, :] = turn_ref[...]
     pose_ref[12:13, :] = kind_ref[...].astype(F32)
     pose_ref[13:16, :] = jnp.zeros((3, GRAINS_DEV), F32)
-    index = jnp.concatenate([first_ref[...], wide(cross_first_ref[...]), export_ref[...]], 1)
     poses = thirds(pose_ref[...])
     thirds_ref[...] = poses
-    got = joined(dot(poses, hot(index, GRAINS_DEV)))
+    got = joined(dot(poses, hot_ref[...]))
     at = iota((16, LANES), 0)
     second, neck = second_ref[...].astype(F32), neck_ref[...]
     cross_second, cross_neck = wide(cross_second_ref[...]).astype(F32), wide(cross_neck_ref[...])
@@ -362,7 +365,7 @@
             shape(16, LANES), shape(16, LANES), shape(16, LANES),
         ),
         scratch_shapes=[pltpu.VMEM(x.shape, x.dtype) for x in sources]
-        + [pltpu.VMEM((16, GRAINS_DEV), F32), pltpu.SemaphoreType.DMA((12,))],
+        + [pltpu.VMEM((16, GRAINS_DEV), F32), pltpu.VMEM((GRAINS_DEV, 3 * LANES), BF16), pltpu.SemaphoreType.DMA((12,))],
         compiler_params=pltpu.CompilerParams(vmem_limit_bytes=60 << 20),
         name="prepare",
     )(*sources)

time: 33.5 us -> 33.2 us (level); the launches traced: 33.7 us -> 32.5 us
  Pallas kernels: 20.2 us -> 19.1 us
    pallas_call x1, Pallas kernels: 10.1 us -> 9.17 us  [on_device(): pl.pallas_call(remote_kernel, out_shape=(shape(3, GRAINS_DEV), shape(3, G...]
where the time goes in v2:
time: 33.2 us; the launch traced here: 32.5 us
  Pallas kernels  19.1 us (58%)
  starting transfers between devices  12.6 us (38%)
  between operations  0.78 us (2%)
    ppermute x5, starting transfers between devices, shifted(): lax.ppermute(array, axis, [(i, (i + by) % devices) for i in range(devices)])  12.6 us
    pallas_call x1, Pallas kernels, on_device(): pl.pallas_call(remote_kernel, out_shape=(shape(3, GRAINS_DEV), shape(3, G...  9.17 us
    pallas_call x1, Pallas kernels, on_device(): pl.pallas_call(local_kernel, out_shape=(shape(8, GRAINS_DEV), shape(4 * S...  7.91 us
    pallas_call x1, Pallas kernels, on_device(): pl.pallas_call(prepare_kernel, in_specs=[pl.BlockSpec(memory_space=pltpu....  1.97 us
  transfers between devices with their start and end apart: 5, of which 0 were waited for; matrix products, arithmetic and copies ran while one was open for 0% of the time, Pallas kernels for 24%

profile of v2, /device:TPU:8, one launch (start us, length us, event | category | flops | bytes accessed | tf_op | source)
XLA Modules:
  0.0 32.5 jit_solution(910688463505231881)
XLA Ops:
  0.6 0.0 copy-start.6
  0.6 2.0 %prepare.1 = (f32[3,1024]{1,0:T(4,128)}, bf16[48,1024]{1,0:T(8,128)(2,1)}, f32[8,128]{1,0:T(8,128)}, f32[32,128]{1,0:T(8,128)}, f32[16,128]{1,0:T(8,128)}, /*index=5*/f32[16,128]{1,0:T(8,128)}, f32[16,128]{1,0:T(8,128)}) custom-call(f32[3,1024]{1,0:T(4,128)} %position_hbm.1, f32[3,1024]{1,0:T(4,128)} %velocity_ref.1, f32[3,1024]{1,0:T(4,128)} %accel_ref.1, ...), custom_call_target="tpu_custom_call" | custom-call | tf_op jit(solution)/shard_map/prepare/pallas_call | solution.py:360
  2.6 0.1 collective-permute-start
  2.7 7.6 %collective-permute-start.1 = (f32[32,128]{1,0:T(8,128)}, f32[32,128]{1,0:T(8,128)S(1)}, u32[]{:S(2)}, u32[]{:S(2)}) collective-permute-start(f32[32,128]{1,0:T(8,128)} %get-tuple-element.19), channel_id=1, source_target_pairs={{0,63},{1,0},{2,1},{3,2},{4,3},{5,4},{6,5},{7,6},{8,7},{9,8},{10,9... | collective-permute-start | bytes 49160 | tf_op jit(solution)/shard_map/ppermute | solution.py:342
  10.3 1.6 %collective-permute-start.2 = (f32[16,128]{1,0:T(8,128)}, f32[16,128]{1,0:T(8,128)S(1)}, u32[]{:S(2)}, u32[]{:S(2)}) collective-permute-start(f32[16,128]{1,0:T(8,128)} %get-tuple-element.20), channel_id=1, source_target_pairs={{0,64},{64,128},{128,192},{192,0},{1,65},{65,129},{129,193},{193,1... | collective-permute-start | bytes 24584 | tf_op jit(solution)/shard_map/ppermute | solution.py:342
  11.9 0.9 %collective-permute-start.3 = (f32[16,128]{1,0:T(8,128)}, f32[16,128]{1,0:T(8,128)S(1)}, u32[]{:S(2)}, u32[]{:S(2)}) collective-permute-start(f32[16,128]{1,0:T(8,128)} %get-tuple-element.21), channel_id=1, source_target_pairs={{0,128},{64,192},{128,0},{192,64},{1,129},{65,193},{129,1},{193,65... | collective-permute-start | bytes 24584 | tf_op jit(solution)/shard_map/ppermute | solution.py:342
  12.8 0.0 copy-start
  12.8 0.0 copy-start.4
  12.8 0.0 copy-start.5
  12.8 2.4 %collective-permute-start.4 = (f32[16,128]{1,0:T(8,128)}, f32[16,128]{1,0:T(8,128)S(1)}, u32[]{:S(2)}, u32[]{:S(2)}) collective-permute-start(f32[16,128]{1,0:T(8,128)} %get-tuple-element.22), channel_id=1, source_target_pairs={{0,192},{64,0},{128,64},{192,128},{1,193},{65,1},{129,65},{193,129... | collective-permute-start | bytes 24584 | tf_op jit(solution)/shard_map/ppermute | solution.py:342
  15.2 0.0 copy-done.6
  15.2 0.1 copy.18.offset_ref
  15.3 0.0 copy-done
  15.3 0.0 copy-done.4
  15.3 0.0 copy-done.5
  15.3 0.0 copy-start.1
  15.3 0.0 copy-start.2
  15.3 0.0 copy-start.3
  15.4 7.9 %local.1 = (f32[8,1024]{1,0:T(8,128)S(1)}, bf16[512,256]{1,0:T(8,128)(2,1)S(1)}) custom-call(bf16[48,1024]{1,0:T(8,128)(2,1)S(1)} %copy-done, f32[8,128]{1,0:T(8,128)S(1)} %copy-done.4, f32[64,3,128]{2,1,0:T(4,128)S(1)} %copy.18.offset_ref, f32[64,128]{1,0:T(8,128)S(1)} %copy-done.5), custom_call_target="tpu_custom_call" | custom-call | flops 4000000000 | bytes 1000000 | tf_op jit(solution)/shard_map/local/pallas_call | solution.py:380
  23.3 0.0 collective-permute-done.2.far1_ref
  23.3 0.0 collective-permute-done.3.far2_ref
  23.3 0.0 collective-permute-done.4.far3_ref
  23.3 0.0 collective-permute-done.before_ref
  23.3 0.0 collective-permute-done.1.after_ref
  23.3 0.0 copy-done.1
  23.4 0.0 copy-done.2
  23.4 0.0 copy-done.3
  23.4 9.2 %remote.1 = (f32[3,1024]{1,0:T(4,128)}, f32[3,1024]{1,0:T(4,128)}) custom-call(bf16[48,1024]{1,0:T(8,128)(2,1)S(1)} %copy-done, f32[8,128]{1,0:T(8,128)S(1)} %copy-done.4, bf16[512,256]{1,0:T(8,128)(2,1)S(1)} %get-tuple-element.17.table_ref, f32[8,1024]{1,0:T(8,128)S(1)} %get-tuple-element.18.local_ref, f32[3,1024]{1,0:T(4,128)S(1)} %copy-done.1, ...), custom_call_target="tpu_custom_call" | custom-call | tf_op jit(solution)/shard_map/remote/pallas_call | solution.py:388
Async XLA Ops:
  0.6 14.6 %copy-start.6 = (f32[64,3,128]{2,0,1:T(8,128)S(1)}, f32[64,3,128]{2,0,1:T(8,128)}, u32[]{:S(2)}) copy-start(f32[64,3,128]{2,0,1:T(8,128)} %param.21) | copy-start | bytes 294916
  2.6 20.7 %collective-permute-start = (f32[32,128]{1,0:T(8,128)}, f32[32,128]{1,0:T(8,128)S(1)}, u32[]{:S(2)}, u32[]{:S(2)}) collective-permute-start(f32[32,128]{1,0:T(8,128)} %get-tuple-element.19), channel_id=1, source_target_pairs={{0,1},{1,2},{2,3},{3,4},{4,5},{5,6},{6,7},{7,8},{8,9},{9,10},{10,1... | collective-permute-start | bytes 49160 | tf_op jit(solution)/shard_map/ppermute | solution.py:342
  2.7 20.6 %collective-permute-start.1 = (f32[32,128]{1,0:T(8,128)}, f32[32,128]{1,0:T(8,128)S(1)}, u32[]{:S(2)}, u32[]{:S(2)}) collective-permute-start(f32[32,128]{1,0:T(8,128)} %get-tuple-element.19), channel_id=1, source_target_pairs={{0,63},{1,0},{2,1},{3,2},{4,3},{5,4},{6,5},{7,6},{8,7},{9,8},{10,9... | collective-permute-start | bytes 49160 | tf_op jit(solution)/shard_map/ppermute | solution.py:342
  10.3 13.0 %collective-permute-start.2 = (f32[16,128]{1,0:T(8,128)}, f32[16,128]{1,0:T(8,128)S(1)}, u32[]{:S(2)}, u32[]{:S(2)}) collective-permute-start(f32[16,128]{1,0:T(8,128)} %get-tuple-element.20), channel_id=1, source_target_pairs={{0,64},{64,128},{128,192},{192,0},{1,65},{65,129},{129,193},{193,1... | collective-permute-start | bytes 24584 | tf_op jit(solution)/shard_map/ppermute | solution.py:342
  11.9 11.4 %collective-permute-start.3 = (f32[16,128]{1,0:T(8,128)}, f32[16,128]{1,0:T(8,128)S(1)}, u32[]{:S(2)}, u32[]{:S(2)}) collective-permute-start(f32[16,128]{1,0:T(8,128)} %get-tuple-element.21), channel_id=1, source_target_pairs={{0,128},{64,192},{128,0},{192,64},{1,129},{65,193},{129,1},{193,65... | collective-permute-start | bytes 24584 | tf_op jit(solution)/shard_map/ppermute | solution.py:342
  12.8 2.5 %copy-start = (bf16[48,1024]{1,0:T(8,128)(2,1)S(1)}, bf16[48,1024]{1,0:T(8,128)(2,1)}, u32[]{:S(2)}) copy-start(bf16[48,1024]{1,0:T(8,128)(2,1)} %get-tuple-element.15.poses_ref) | copy-start | bytes 294916
  12.8 2.5 %copy-start.4 = (f32[8,128]{1,0:T(8,128)S(1)}, f32[8,128]{1,0:T(8,128)}, u32[]{:S(2)}) copy-start(f32[8,128]{1,0:T(8,128)} %get-tuple-element.16.list_ref) | copy-start | bytes 12292
  12.8 2.5 %copy-start.5 = (f32[64,128]{1,0:T(8,128)S(1)}, f32[64,128]{1,0:T(8,128)}, u32[]{:S(2)}) copy-start(f32[64,128]{1,0:T(8,128)} %radius_ref.1) | copy-start | bytes 98308
  12.8 10.5 %collective-permute-start.4 = (f32[16,128]{1,0:T(8,128)}, f32[16,128]{1,0:T(8,128)S(1)}, u32[]{:S(2)}, u32[]{:S(2)}) collective-permute-start(f32[16,128]{1,0:T(8,128)} %get-tuple-element.22), channel_id=1, source_target_pairs={{0,192},{64,0},{128,64},{192,128},{1,193},{65,1},{129,65},{193,129... | collective-permute-start | bytes 24584 | tf_op jit(solution)/shard_map/ppermute | solution.py:342
  15.3 8.0 %copy-start.1 = (f32[3,1024]{1,0:T(4,128)S(1)}, f32[3,1024]{1,0:T(4,128)}, u32[]{:S(2)}) copy-start(f32[3,1024]{1,0:T(4,128)} %velocity_ref.1) | copy-start | bytes 36868
  15.3 8.0 %copy-start.2 = (f32[3,1024]{1,0:T(4,128)S(1)}, f32[3,1024]{1,0:T(4,128)}, u32[]{:S(2)}) copy-start(f32[3,1024]{1,0:T(4,128)} %accel_ref.1) | copy-start | bytes 36868
  15.3 8.0 %copy-start.3 = (f32[3,1024]{1,0:T(4,128)S(1)}, f32[3,1024]{1,0:T(4,128)}, u32[]{:S(2)}) copy-start(f32[3,1024]{1,0:T(4,128)} %spin_ref.1) | copy-start | bytes 36868

commit v3 on v2

--- a/solution.py
+++ b/solution.py
@@ -120,7 +120,7 @@
         return tuple(out)
 
     zero = jnp.zeros((8, LANES), F32)
-    sums = lax.fori_loop(0, SUB, step, ((zero,) * 3,) * len(u), unroll=32)
+    sums = lax.fori_loop(0, SUB, step, ((zero,) * 3,) * len(u), unroll=64)
     rows = [zero] * 6
     for one, g in zip(u, sums):
         for c in range(3):

time: 33.2 us -> 33.5 us (level); the launches traced: 32.5 us -> 33.2 us
  Pallas kernels: 19.1 us -> 19.7 us
    pallas_call x1, Pallas kernels: 9.17 us -> 9.91 us  [on_device(): pl.pallas_call(remote_kernel, out_shape=(shape(3, GRAINS_DEV), shape(3, G...]
where the time goes in v3:
time: 33.5 us; the launch traced here: 33.2 us
  Pallas kernels  19.7 us (59%)
  starting transfers between devices  12.6 us (38%)
  between operations  0.78 us (2%)
    ppermute x5, starting transfers between devices, shifted(): lax.ppermute(array, axis, [(i, (i + by) % devices) for i in range(devices)])  12.6 us
    pallas_call x1, Pallas kernels, on_device(): pl.pallas_call(remote_kernel, out_shape=(shape(3, GRAINS_DEV), shape(3, G...  9.91 us
    pallas_call x1, Pallas kernels, on_device(): pl.pallas_call(local_kernel, out_shape=(shape(8, GRAINS_DEV), shape(4 * S...  7.86 us
    pallas_call x1, Pallas kernels, on_device(): pl.pallas_call(prepare_kernel, in_specs=[pl.BlockSpec(memory_space=pltpu....  1.97 us
  transfers between devices with their start and end apart: 5, of which 0 were waited for; matrix products, arithmetic and copies ran while one was open for 0% of the time, Pallas kernels for 24%

profile of v3, /device:TPU:8, one launch (start us, length us, event | category | flops | bytes accessed | tf_op | source)
XLA Modules:
  0.0 33.2 jit_solution(17349221525386009301)
XLA Ops:
  0.6 0.0 copy-start.6
  0.6 2.0 %prepare.1 = (f32[3,1024]{1,0:T(4,128)}, bf16[48,1024]{1,0:T(8,128)(2,1)}, f32[8,128]{1,0:T(8,128)}, f32[32,128]{1,0:T(8,128)}, f32[16,128]{1,0:T(8,128)}, /*index=5*/f32[16,128]{1,0:T(8,128)}, f32[16,128]{1,0:T(8,128)}) custom-call(f32[3,1024]{1,0:T(4,128)} %position_hbm.1, f32[3,1024]{1,0:T(4,128)} %velocity_ref.1, f32[3,1024]{1,0:T(4,128)} %accel_ref.1, ...), custom_call_target="tpu_custom_call" | custom-call | tf_op jit(solution)/shard_map/prepare/pallas_call | solution.py:360
  2.6 0.1 collective-permute-start
  2.7 7.6 %collective-permute-start.1 = (f32[32,128]{1,0:T(8,128)}, f32[32,128]{1,0:T(8,128)S(1)}, u32[]{:S(2)}, u32[]{:S(2)}) collective-permute-start(f32[32,128]{1,0:T(8,128)} %get-tuple-element.19), channel_id=1, source_target_pairs={{0,63},{1,0},{2,1},{3,2},{4,3},{5,4},{6,5},{7,6},{8,7},{9,8},{10,9... | collective-permute-start | bytes 49160 | tf_op jit(solution)/shard_map/ppermute | solution.py:342
  10.3 1.6 %collective-permute-start.2 = (f32[16,128]{1,0:T(8,128)}, f32[16,128]{1,0:T(8,128)S(1)}, u32[]{:S(2)}, u32[]{:S(2)}) collective-permute-start(f32[16,128]{1,0:T(8,128)} %get-tuple-element.20), channel_id=1, source_target_pairs={{0,64},{64,128},{128,192},{192,0},{1,65},{65,129},{129,193},{193,1... | collective-permute-start | bytes 24584 | tf_op jit(solution)/shard_map/ppermute | solution.py:342
  11.9 0.9 %collective-permute-start.3 = (f32[16,128]{1,0:T(8,128)}, f32[16,128]{1,0:T(8,128)S(1)}, u32[]{:S(2)}, u32[]{:S(2)}) collective-permute-start(f32[16,128]{1,0:T(8,128)} %get-tuple-element.21), channel_id=1, source_target_pairs={{0,128},{64,192},{128,0},{192,64},{1,129},{65,193},{129,1},{193,65... | collective-permute-start | bytes 24584 | tf_op jit(solution)/shard_map/ppermute | solution.py:342
  12.8 0.0 copy-start
  12.8 0.0 copy-start.4
  12.8 0.0 copy-start.5
  12.8 2.4 %collective-permute-start.4 = (f32[16,128]{1,0:T(8,128)}, f32[16,128]{1,0:T(8,128)S(1)}, u32[]{:S(2)}, u32[]{:S(2)}) collective-permute-start(f32[16,128]{1,0:T(8,128)} %get-tuple-element.22), channel_id=1, source_target_pairs={{0,192},{64,0},{128,64},{192,128},{1,193},{65,1},{129,65},{193,129... | collective-permute-start | bytes 24584 | tf_op jit(solution)/shard_map/ppermute | solution.py:342
  15.2 0.0 copy-done.6
  15.2 0.1 copy.18.offset_ref
  15.3 0.0 copy-done
  15.3 0.0 copy-done.4
  15.3 0.0 copy-done.5
  15.3 0.0 copy-start.1
  15.3 0.0 copy-start.2
  15.3 0.0 copy-start.3
  15.4 7.9 %local.1 = (f32[8,1024]{1,0:T(8,128)S(1)}, bf16[512,256]{1,0:T(8,128)(2,1)S(1)}) custom-call(bf16[48,1024]{1,0:T(8,128)(2,1)S(1)} %copy-done, f32[8,128]{1,0:T(8,128)S(1)} %copy-done.4, f32[64,3,128]{2,1,0:T(4,128)S(1)} %copy.18.offset_ref, f32[64,128]{1,0:T(8,128)S(1)} %copy-done.5), custom_call_target="tpu_custom_call" | custom-call | flops 4000000000 | bytes 1000000 | tf_op jit(solution)/shard_map/local/pallas_call | solution.py:380
  23.2 0.0 collective-permute-done.2.far1_ref
  23.2 0.0 collective-permute-done.3.far2_ref
  23.3 0.0 collective-permute-done.4.far3_ref
  23.3 0.0 collective-permute-done.before_ref
  23.3 0.0 collective-permute-done.1.after_ref
  23.3 0.0 copy-done.1
  23.3 0.0 copy-done.2
  23.3 0.0 copy-done.3
  23.3 9.9 %remote.1 = (f32[3,1024]{1,0:T(4,128)}, f32[3,1024]{1,0:T(4,128)}) custom-call(bf16[48,1024]{1,0:T(8,128)(2,1)S(1)} %copy-done, f32[8,128]{1,0:T(8,128)S(1)} %copy-done.4, bf16[512,256]{1,0:T(8,128)(2,1)S(1)} %get-tuple-element.17.table_ref, f32[8,1024]{1,0:T(8,128)S(1)} %get-tuple-element.18.local_ref, f32[3,1024]{1,0:T(4,128)S(1)} %copy-done.1, ...), custom_call_target="tpu_custom_call" | custom-call | tf_op jit(solution)/shard_map/remote/pallas_call | solution.py:388
Async XLA Ops:
  0.6 14.6 %copy-start.6 = (f32[64,3,128]{2,0,1:T(8,128)S(1)}, f32[64,3,128]{2,0,1:T(8,128)}, u32[]{:S(2)}) copy-start(f32[64,3,128]{2,0,1:T(8,128)} %param.21) | copy-start | bytes 294916
  2.6 20.6 %collective-permute-start = (f32[32,128]{1,0:T(8,128)}, f32[32,128]{1,0:T(8,128)S(1)}, u32[]{:S(2)}, u32[]{:S(2)}) collective-permute-start(f32[32,128]{1,0:T(8,128)} %get-tuple-element.19), channel_id=1, source_target_pairs={{0,1},{1,2},{2,3},{3,4},{4,5},{5,6},{6,7},{7,8},{8,9},{9,10},{10,1... | collective-permute-start | bytes 49160 | tf_op jit(solution)/shard_map/ppermute | solution.py:342
  2.7 20.6 %collective-permute-start.1 = (f32[32,128]{1,0:T(8,128)}, f32[32,128]{1,0:T(8,128)S(1)}, u32[]{:S(2)}, u32[]{:S(2)}) collective-permute-start(f32[32,128]{1,0:T(8,128)} %get-tuple-element.19), channel_id=1, source_target_pairs={{0,63},{1,0},{2,1},{3,2},{4,3},{5,4},{6,5},{7,6},{8,7},{9,8},{10,9... | collective-permute-start | bytes 49160 | tf_op jit(solution)/shard_map/ppermute | solution.py:342
  10.3 13.0 %collective-permute-start.2 = (f32[16,128]{1,0:T(8,128)}, f32[16,128]{1,0:T(8,128)S(1)}, u32[]{:S(2)}, u32[]{:S(2)}) collective-permute-start(f32[16,128]{1,0:T(8,128)} %get-tuple-element.20), channel_id=1, source_target_pairs={{0,64},{64,128},{128,192},{192,0},{1,65},{65,129},{129,193},{193,1... | collective-permute-start | bytes 24584 | tf_op jit(solution)/shard_map/ppermute | solution.py:342
  11.9 11.4 %collective-permute-start.3 = (f32[16,128]{1,0:T(8,128)}, f32[16,128]{1,0:T(8,128)S(1)}, u32[]{:S(2)}, u32[]{:S(2)}) collective-permute-start(f32[16,128]{1,0:T(8,128)} %get-tuple-element.21), channel_id=1, source_target_pairs={{0,128},{64,192},{128,0},{192,64},{1,129},{65,193},{129,1},{193,65... | collective-permute-start | bytes 24584 | tf_op jit(solution)/shard_map/ppermute | solution.py:342
  12.8 2.5 %copy-start = (bf16[48,1024]{1,0:T(8,128)(2,1)S(1)}, bf16[48,1024]{1,0:T(8,128)(2,1)}, u32[]{:S(2)}) copy-start(bf16[48,1024]{1,0:T(8,128)(2,1)} %get-tuple-element.15.poses_ref) | copy-start | bytes 294916
  12.8 2.5 %copy-start.4 = (f32[8,128]{1,0:T(8,128)S(1)}, f32[8,128]{1,0:T(8,128)}, u32[]{:S(2)}) copy-start(f32[8,128]{1,0:T(8,128)} %get-tuple-element.16.list_ref) | copy-start | bytes 12292
  12.8 2.5 %copy-start.5 = (f32[64,128]{1,0:T(8,128)S(1)}, f32[64,128]{1,0:T(8,128)}, u32[]{:S(2)}) copy-start(f32[64,128]{1,0:T(8,128)} %radius_ref.1) | copy-start | bytes 98308
  12.8 10.5 %collective-permute-start.4 = (f32[16,128]{1,0:T(8,128)}, f32[16,128]{1,0:T(8,128)S(1)}, u32[]{:S(2)}, u32[]{:S(2)}) collective-permute-start(f32[16,128]{1,0:T(8,128)} %get-tuple-element.22), channel_id=1, source_target_pairs={{0,192},{64,0},{128,64},{192,128},{1,193},{65,1},{129,65},{193,129... | collective-permute-start | bytes 24584 | tf_op jit(solution)/shard_map/ppermute | solution.py:342
  15.3 8.0 %copy-start.1 = (f32[3,1024]{1,0:T(4,128)S(1)}, f32[3,1024]{1,0:T(4,128)}, u32[]{:S(2)}) copy-start(f32[3,1024]{1,0:T(4,128)} %velocity_ref.1) | copy-start | bytes 36868
  15.3 8.0 %copy-start.2 = (f32[3,1024]{1,0:T(4,128)S(1)}, f32[3,1024]{1,0:T(4,128)}, u32[]{:S(2)}) copy-start(f32[3,1024]{1,0:T(4,128)} %accel_ref.1) | copy-start | bytes 36868
  15.3 8.0 %copy-start.3 = (f32[3,1024]{1,0:T(4,128)S(1)}, f32[3,1024]{1,0:T(4,128)}, u32[]{:S(2)}) copy-start(f32[3,1024]{1,0:T(4,128)} %spin_ref.1) | copy-start | bytes 36868
